TPU v7x, 256 devices: a whole 4x4x8 slice. The times are simulated.
256 devices in a mesh: ta: 8 (over y, z_lo), gx: 4 (over x), gy: 8 (over z_hi, core).
Axes of the slice: x: 4, y: 4, z: 8 (z_hi: 4, z_lo: 2; z = z_hi * 2 + z_lo), core: 2. Of those that a mesh axis runs over, the one named last changes fastest.
Arguments:
- start_states: float32 [8, 256, 4096], P('ta', 'gx', 'gy'), may hold values from -6 to 6
- conduct: float32 [256, 4096], P('gx', 'gy'), may hold values from 0.5 to 2
- velocity: float32 [2, 256, 4096], P(None, 'gx', 'gy'), may hold values from -1 to 1
Outputs:
- end_states: float32 [8, 256, 4096], P('ta', 'gx', 'gy')
All inputs are finite; a program needn't handle non-finite values.
Results may differ from a plain program's by a relative error of at most 0.00002.
Values sent between devices are 32-bit elements; how exact they have to be, the bound alone decides.
A program may use at most 64 MiB of HBM per device.

v0:
```python
import jax
import jax.numpy as jnp
from jax import lax
from jax.sharding import PartitionSpec as P

FINE = 2


def with_halo(block, sides, width):
    for axis, dim in sides:
        count = lax.axis_size(axis)
        forward = [(i, i + 1) for i in range(count - 1)]
        backward = [(target, source) for source, target in forward]
        low = lax.ppermute(
            lax.slice_in_dim(block, block.shape[dim] - width, None, axis=dim), axis, forward
        )
        high = lax.ppermute(lax.slice_in_dim(block, 0, width, axis=dim), axis, backward)
        block = jnp.concatenate([low, block, high], axis=dim)
    return block


def shifted(value, axis, steps):
    count = lax.axis_size(axis)
    first, last = (max(0, -steps), min(count, count - steps))
    return lax.ppermute(value, axis, [(source, source + steps) for source in range(first, last)])


def element_rates(padded, kel, vxel, vyel):
    corner_a = padded[:-1, :-1]
    corner_b = padded[1:, :-1]
    corner_c = padded[:-1, 1:]
    corner_d = padded[1:, 1:]
    advect = 0.25 * (
        vxel * (0.5 * (corner_b + corner_d - corner_a - corner_c))
        + vyel * (0.5 * (corner_c + corner_d - corner_a - corner_b))
    )
    stiff = kel / 6.0
    rate_a = stiff * (4.0 * corner_a - corner_b - corner_c - 2.0 * corner_d) + advect
    rate_b = stiff * (4.0 * corner_b - corner_a - corner_d - 2.0 * corner_c) + advect
    rate_c = stiff * (4.0 * corner_c - corner_a - corner_d - 2.0 * corner_b) + advect
    rate_d = stiff * (4.0 * corner_d - corner_b - corner_c - 2.0 * corner_a) + advect
    return rate_a[1:, 1:] + rate_b[:-1, 1:] + rate_c[1:, :-1] + rate_d[:-1, :-1]


def element_means(padded):
    return 0.25 * (
        padded[:, :-1, :-1] + padded[:, 1:, :-1] + padded[:, :-1, 1:] + padded[:, 1:, 1:]
    )


def margin_one(field):
    return with_halo(field, (("gx", 0), ("gy", 1)), 1)


def local(start_states, conduct, velocity):
    coeffs = jnp.concatenate([conduct[None], velocity], axis=0)
    padded_coeffs = with_halo(coeffs, (("gx", 1), ("gy", 2)), 2)
    outer = element_means(padded_coeffs)
    inner = outer[:, 1:-1, 1:-1]

    def heun_step(field, step):
        first = element_rates(margin_one(field), inner[0], inner[1], inner[2])
        middle = field - step * first
        second = element_rates(margin_one(middle), inner[0], inner[1], inner[2])
        return field - 0.5 * step * (first + second)

    own_state = start_states[0]
    fine_state = own_state
    for inner_step in range(FINE):
        fine_state = heun_step(fine_state, 0.1)
    coarse_own = heun_step(own_state, 0.2)
    delta = fine_state - coarse_own
    sections = lax.axis_size("ta")
    my_section = lax.axis_index("ta")
    result = jnp.zeros_like(own_state)
    current = own_state
    for section in range(sections):
        if section == 0:
            advanced = coarse_own
        else:
            advanced = heun_step(current, 0.2)
        candidate = advanced + delta
        result = jnp.where(my_section == section, candidate, result)
        if section + 1 < sections:
            current = shifted(candidate, "ta", 1)
    return result[None]


def solution(mesh):
    in_specs = (P("ta", "gx", "gy"), P("gx", "gy"), P(None, "gx", "gy"))
    out_specs = P("ta", "gx", "gy")
    return jax.shard_map(local, mesh=mesh, in_specs=in_specs, out_specs=out_specs, check_vma=False)
```

profile of v0, /device:TPU:79, one launch (start us, length us, event | category | flops | bytes accessed | tf_op | source)
XLA Modules:
  0.0 405.5 jit_solution(13838700265348087434)
XLA Ops:
  10.9 7.5 %collective-permute-start.6 = (f32[66,1]{1,0:T(8,128)S(1)}, f32[66,1]{1,0:T(8,128)S(1)}, u32[]{:S(2)}, u32[]{:S(2)}) collective-permute-start(f32[66,1]{1,0:T(8,128)S(1)} %get-tuple-element.197), channel_id=1, source_target_pairs={{0,1},{1,2},{2,3},{3,4},{4,5},{5,6},{6,7},{8,9},{9,10},{10,11},{11... | collective-permute-start | bytes 800 | tf_op jit(solution)/shard_map/ppermute | solution.py:14
  22.4 5.8 %collective-permute-start.2 = (f32[3,68,2]{2,1,0:T(8,128)S(1)}, f32[3,68,2]{2,1,0:T(8,128)S(1)}, u32[]{:S(2)}, u32[]{:S(2)}) collective-permute-start(f32[3,68,2]{2,1,0:T(8,128)S(1)} %get-tuple-element.27), channel_id=1, source_target_pairs={{0,1},{1,2},{2,3},{3,4},{4,5},{5,6},{6,7},{8,9},{9,10},{10,11},{11... | collective-permute-start | bytes 4904 | tf_op jit(solution)/shard_map/ppermute | solution.py:14
  40.1 8.0 %collective-permute-start.14 = (f32[66,1]{1,0:T(8,128)S(1)}, f32[66,1]{1,0:T(8,128)S(1)}, u32[]{:S(2)}, u32[]{:S(2)}) collective-permute-start(f32[66,1]{1,0:T(8,128)S(1)} %get-tuple-element.189), channel_id=1, source_target_pairs={{0,1},{1,2},{2,3},{3,4},{4,5},{5,6},{6,7},{8,9},{9,10},{10,11},{11... | collective-permute-start | bytes 800 | tf_op jit(solution)/shard_map/ppermute | solution.py:14
  50.0 5.4 %collective-permute-done.15 = f32[66,1]{1,0:T(8,128)S(1)} collective-permute-done((f32[66,1]{1,0:T(8,128)S(1)}, f32[66,1]{1,0:T(8,128)S(1)}, u32[]{:S(2)}, u32[]{:S(2)}) %collective-permute-start.15) | collective-permute-done | bytes 296 | tf_op jit(solution)/shard_map/ppermute | solution.py:17
  78.0 6.4 %collective-permute-start.10 = (f32[66,1]{1,0:T(8,128)S(1)}, f32[66,1]{1,0:T(8,128)S(1)}, u32[]{:S(2)}, u32[]{:S(2)}) collective-permute-start(f32[66,1]{1,0:T(8,128)S(1)} %get-tuple-element.193), channel_id=1, source_target_pairs={{0,1},{1,2},{2,3},{3,4},{4,5},{5,6},{6,7},{8,9},{9,10},{10,11},{11... | collective-permute-start | bytes 800 | tf_op jit(solution)/shard_map/ppermute | solution.py:14
  86.5 5.7 %collective-permute-start.22 = (f32[66,1]{1,0:T(8,128)S(1)}, f32[66,1]{1,0:T(8,128)S(1)}, u32[]{:S(2)}, u32[]{:S(2)}) collective-permute-start(f32[66,1]{1,0:T(8,128)S(1)} %get-tuple-element.181), channel_id=1, source_target_pairs={{0,1},{1,2},{2,3},{3,4},{4,5},{5,6},{6,7},{8,9},{9,10},{10,11},{11... | collective-permute-start | bytes 800 | tf_op jit(solution)/shard_map/ppermute | solution.py:14
  94.4 5.3 %collective-permute-done.23 = f32[66,1]{1,0:T(8,128)S(1)} collective-permute-done((f32[66,1]{1,0:T(8,128)S(1)}, f32[66,1]{1,0:T(8,128)S(1)}, u32[]{:S(2)}, u32[]{:S(2)}) %collective-permute-start.23) | collective-permute-done | bytes 296 | tf_op jit(solution)/shard_map/ppermute | solution.py:17
  122.7 5.4 %collective-permute-done.28 = f32[66,1]{1,0:T(8,128)S(1)} collective-permute-done((f32[66,1]{1,0:T(8,128)S(1)}, f32[66,1]{1,0:T(8,128)S(1)}, u32[]{:S(2)}, u32[]{:S(2)}) %collective-permute-start.28) | collective-permute-done | bytes 296 | tf_op jit(solution)/shard_map/ppermute | solution.py:17
  140.3 5.4 %collective-permute-done.32 = f32[66,1]{1,0:T(8,128)S(1)} collective-permute-done((f32[66,1]{1,0:T(8,128)S(1)}, f32[66,1]{1,0:T(8,128)S(1)}, u32[]{:S(2)}, u32[]{:S(2)}) %collective-permute-start.32) | collective-permute-done | bytes 296 | tf_op jit(solution)/shard_map/ppermute | solution.py:17
  165.7 5.6 %collective-permute-done.37 = f32[66,1]{1,0:T(8,128)S(1)} collective-permute-done((f32[66,1]{1,0:T(8,128)S(1)}, f32[66,1]{1,0:T(8,128)S(1)}, u32[]{:S(2)}, u32[]{:S(2)}) %collective-permute-start.37) | collective-permute-done | bytes 296 | tf_op jit(solution)/shard_map/ppermute | solution.py:17
  183.4 5.6 %collective-permute-done.41 = f32[66,1]{1,0:T(8,128)S(1)} collective-permute-done((f32[66,1]{1,0:T(8,128)S(1)}, f32[66,1]{1,0:T(8,128)S(1)}, u32[]{:S(2)}, u32[]{:S(2)}) %collective-permute-start.41) | collective-permute-done | bytes 296 | tf_op jit(solution)/shard_map/ppermute | solution.py:17
  208.9 5.3 %collective-permute-done.46 = f32[66,1]{1,0:T(8,128)S(1)} collective-permute-done((f32[66,1]{1,0:T(8,128)S(1)}, f32[66,1]{1,0:T(8,128)S(1)}, u32[]{:S(2)}, u32[]{:S(2)}) %collective-permute-start.46) | collective-permute-done | bytes 296 | tf_op jit(solution)/shard_map/ppermute | solution.py:17
  226.4 5.4 %collective-permute-done.50 = f32[66,1]{1,0:T(8,128)S(1)} collective-permute-done((f32[66,1]{1,0:T(8,128)S(1)}, f32[66,1]{1,0:T(8,128)S(1)}, u32[]{:S(2)}, u32[]{:S(2)}) %collective-permute-start.50) | collective-permute-done | bytes 296 | tf_op jit(solution)/shard_map/ppermute | solution.py:17
  234.6 4.7 %collective-permute-done.51 = f32[64,512]{1,0:T(8,128)S(1)} collective-permute-done((f32[64,512]{1,0:T(8,128)S(1)}, f32[64,512]{1,0:T(8,128)S(1)}, u32[]{:S(2)}, u32[]{:S(2)}) %collective-permute-start.51) | collective-permute-done | bytes 131104 | tf_op jit(solution)/shard_map/ppermute | solution.py:25
  251.8 5.4 %collective-permute-done.55 = f32[66,1]{1,0:T(8,128)S(1)} collective-permute-done((f32[66,1]{1,0:T(8,128)S(1)}, f32[66,1]{1,0:T(8,128)S(1)}, u32[]{:S(2)}, u32[]{:S(2)}) %collective-permute-start.55) | collective-permute-done | bytes 296 | tf_op jit(solution)/shard_map/ppermute | solution.py:17
  269.4 5.4 %collective-permute-done.59 = f32[66,1]{1,0:T(8,128)S(1)} collective-permute-done((f32[66,1]{1,0:T(8,128)S(1)}, f32[66,1]{1,0:T(8,128)S(1)}, u32[]{:S(2)}, u32[]{:S(2)}) %collective-permute-start.59) | collective-permute-done | bytes 296 | tf_op jit(solution)/shard_map/ppermute | solution.py:17
  277.6 4.7 %collective-permute-done.60 = f32[64,512]{1,0:T(8,128)S(1)} collective-permute-done((f32[64,512]{1,0:T(8,128)S(1)}, f32[64,512]{1,0:T(8,128)S(1)}, u32[]{:S(2)}, u32[]{:S(2)}) %collective-permute-start.60) | collective-permute-done | bytes 131104 | tf_op jit(solution)/shard_map/ppermute | solution.py:25
  294.8 5.4 %collective-permute-done.64 = f32[66,1]{1,0:T(8,128)S(1)} collective-permute-done((f32[66,1]{1,0:T(8,128)S(1)}, f32[66,1]{1,0:T(8,128)S(1)}, u32[]{:S(2)}, u32[]{:S(2)}) %collective-permute-start.64) | collective-permute-done | bytes 296 | tf_op jit(solution)/shard_map/ppermute | solution.py:17
  312.4 5.4 %collective-permute-done.68 = f32[66,1]{1,0:T(8,128)S(1)} collective-permute-done((f32[66,1]{1,0:T(8,128)S(1)}, f32[66,1]{1,0:T(8,128)S(1)}, u32[]{:S(2)}, u32[]{:S(2)}) %collective-permute-start.68) | collective-permute-done | bytes 296 | tf_op jit(solution)/shard_map/ppermute | solution.py:17
  320.7 4.7 %collective-permute-done.69 = f32[64,512]{1,0:T(8,128)S(1)} collective-permute-done((f32[64,512]{1,0:T(8,128)S(1)}, f32[64,512]{1,0:T(8,128)S(1)}, u32[]{:S(2)}, u32[]{:S(2)}) %collective-permute-start.69) | collective-permute-done | bytes 131104 | tf_op jit(solution)/shard_map/ppermute | solution.py:25
  337.8 5.4 %collective-permute-done.73 = f32[66,1]{1,0:T(8,128)S(1)} collective-permute-done((f32[66,1]{1,0:T(8,128)S(1)}, f32[66,1]{1,0:T(8,128)S(1)}, u32[]{:S(2)}, u32[]{:S(2)}) %collective-permute-start.73) | collective-permute-done | bytes 296 | tf_op jit(solution)/shard_map/ppermute | solution.py:17
  355.5 5.4 %collective-permute-done.77 = f32[66,1]{1,0:T(8,128)S(1)} collective-permute-done((f32[66,1]{1,0:T(8,128)S(1)}, f32[66,1]{1,0:T(8,128)S(1)}, u32[]{:S(2)}, u32[]{:S(2)}) %collective-permute-start.77) | collective-permute-done | bytes 296 | tf_op jit(solution)/shard_map/ppermute | solution.py:17
  380.8 5.4 %collective-permute-done.82 = f32[66,1]{1,0:T(8,128)S(1)} collective-permute-done((f32[66,1]{1,0:T(8,128)S(1)}, f32[66,1]{1,0:T(8,128)S(1)}, u32[]{:S(2)}, u32[]{:S(2)}) %collective-permute-start.82) | collective-permute-done | bytes 296 | tf_op jit(solution)/shard_map/ppermute | solution.py:17
  398.5 5.4 %collective-permute-done.86 = f32[66,1]{1,0:T(8,128)S(1)} collective-permute-done((f32[66,1]{1,0:T(8,128)S(1)}, f32[66,1]{1,0:T(8,128)S(1)}, u32[]{:S(2)}, u32[]{:S(2)}) %collective-permute-start.86) | collective-permute-done | bytes 296 | tf_op jit(solution)/shard_map/ppermute | solution.py:17
  (255 shorter events, 269.5 us)
Async XLA Ops:
  0.7 10.1 %collective-permute-start.5 = (f32[1,512]{1,0:T(1,128)S(1)}, f32[1,512]{1,0:T(1,128)S(1)}, u32[]{:S(2)}, u32[]{:S(2)}) collective-permute-start(f32[1,512]{1,0:T(1,128)S(1)} %get-tuple-element.236), channel_id=1, source_target_pairs={{8,0},{16,8},{24,16},{9,1},{17,9},{25,17},{10,2},{18,10},{26,18},{... | collective-permute-start | bytes 6152 | tf_op jit(solution)/shard_map/ppermute | solution.py:17
  3.2 7.6 %collective-permute-start.4 = (f32[1,512]{1,0:T(1,128)S(1)}, f32[1,512]{1,0:T(1,128)S(1)}, u32[]{:S(2)}, u32[]{:S(2)}) collective-permute-start(f32[1,512]{1,0:T(1,128)S(1)} %get-tuple-element.235), channel_id=1, source_target_pairs={{0,8},{8,16},{16,24},{1,9},{9,17},{17,25},{2,10},{10,18},{18,26},{... | collective-permute-start | bytes 6152 | tf_op jit(solution)/shard_map/ppermute | solution.py:14
  5.4 15.0 %collective-permute-start.1 = (f32[3,2,512]{2,1,0:T(2,128)S(1)}, f32[3,2,512]{2,1,0:T(2,128)S(1)}, u32[]{:S(2)}, u32[]{:S(2)}) collective-permute-start(f32[3,2,512]{2,1,0:T(2,128)S(1)} %get-tuple-element.30), channel_id=1, source_target_pairs={{8,0},{16,8},{24,16},{9,1},{17,9},{25,17},{10,2},{18,10},{26,18},{... | collective-permute-start | bytes 36872 | tf_op jit(solution)/shard_map/ppermute | solution.py:17
  9.5 10.9 %collective-permute-start = (f32[3,2,512]{2,1,0:T(2,128)S(1)}, f32[3,2,512]{2,1,0:T(2,128)S(1)}, u32[]{:S(2)}, u32[]{:S(2)}) collective-permute-start(f32[3,2,512]{2,1,0:T(2,128)S(1)} %get-tuple-element.29), channel_id=1, source_target_pairs={{0,8},{8,16},{16,24},{1,9},{9,17},{17,25},{2,10},{10,18},{18,26},{... | collective-permute-start | bytes 36872 | tf_op jit(solution)/shard_map/ppermute | solution.py:14
  10.9 17.3 %collective-permute-start.6 = (f32[66,1]{1,0:T(8,128)S(1)}, f32[66,1]{1,0:T(8,128)S(1)}, u32[]{:S(2)}, u32[]{:S(2)}) collective-permute-start(f32[66,1]{1,0:T(8,128)S(1)} %get-tuple-element.197), channel_id=1, source_target_pairs={{0,1},{1,2},{2,3},{3,4},{4,5},{5,6},{6,7},{8,9},{9,10},{10,11},{11... | collective-permute-start | bytes 800 | tf_op jit(solution)/shard_map/ppermute | solution.py:14
  18.4 9.8 %collective-permute-start.7 = (f32[66,1]{1,0:T(8,128)S(1)}, f32[66,1]{1,0:T(8,128)S(1)}, u32[]{:S(2)}, u32[]{:S(2)}) collective-permute-start(f32[66,1]{1,0:T(8,128)S(1)} %get-tuple-element.198), channel_id=1, source_target_pairs={{1,0},{2,1},{3,2},{4,3},{5,4},{6,5},{7,6},{9,8},{10,9},{11,10},{12... | collective-permute-start | bytes 800 | tf_op jit(solution)/shard_map/ppermute | solution.py:17
  20.5 9.4 %collective-permute-start.3 = (f32[3,68,2]{2,1,0:T(8,128)S(1)}, f32[3,68,2]{2,1,0:T(8,128)S(1)}, u32[]{:S(2)}, u32[]{:S(2)}) collective-permute-start(f32[3,68,2]{2,1,0:T(8,128)S(1)} %get-tuple-element.28), channel_id=1, source_target_pairs={{1,0},{2,1},{3,2},{4,3},{5,4},{6,5},{7,6},{9,8},{10,9},{11,10},{12... | collective-permute-start | bytes 4904 | tf_op jit(solution)/shard_map/ppermute | solution.py:17
  22.4 7.5 %collective-permute-start.2 = (f32[3,68,2]{2,1,0:T(8,128)S(1)}, f32[3,68,2]{2,1,0:T(8,128)S(1)}, u32[]{:S(2)}, u32[]{:S(2)}) collective-permute-start(f32[3,68,2]{2,1,0:T(8,128)S(1)} %get-tuple-element.27), channel_id=1, source_target_pairs={{0,1},{1,2},{2,3},{3,4},{4,5},{5,6},{6,7},{8,9},{9,10},{10,11},{11... | collective-permute-start | bytes 4904 | tf_op jit(solution)/shard_map/ppermute | solution.py:14
  40.1 9.9 %collective-permute-start.14 = (f32[66,1]{1,0:T(8,128)S(1)}, f32[66,1]{1,0:T(8,128)S(1)}, u32[]{:S(2)}, u32[]{:S(2)}) collective-permute-start(f32[66,1]{1,0:T(8,128)S(1)} %get-tuple-element.189), channel_id=1, source_target_pairs={{0,1},{1,2},{2,3},{3,4},{4,5},{5,6},{6,7},{8,9},{9,10},{10,11},{11... | collective-permute-start | bytes 800 | tf_op jit(solution)/shard_map/ppermute | solution.py:14
  48.1 7.4 %collective-permute-start.15 = (f32[66,1]{1,0:T(8,128)S(1)}, f32[66,1]{1,0:T(8,128)S(1)}, u32[]{:S(2)}, u32[]{:S(2)}) collective-permute-start(f32[66,1]{1,0:T(8,128)S(1)} %get-tuple-element.190), channel_id=1, source_target_pairs={{1,0},{2,1},{3,2},{4,3},{5,4},{6,5},{7,6},{9,8},{10,9},{11,10},{12... | collective-permute-start | bytes 800 | tf_op jit(solution)/shard_map/ppermute | solution.py:17
  62.9 8.7 %collective-permute-start.18 = (f32[66,1]{1,0:T(8,128)S(1)}, f32[66,1]{1,0:T(8,128)S(1)}, u32[]{:S(2)}, u32[]{:S(2)}) collective-permute-start(f32[66,1]{1,0:T(8,128)S(1)} %get-tuple-element.185), channel_id=1, source_target_pairs={{0,1},{1,2},{2,3},{3,4},{4,5},{5,6},{6,7},{8,9},{9,10},{10,11},{11... | collective-permute-start | bytes 800 | tf_op jit(solution)/shard_map/ppermute | solution.py:14
  66.2 7.4 %collective-permute-start.19 = (f32[66,1]{1,0:T(8,128)S(1)}, f32[66,1]{1,0:T(8,128)S(1)}, u32[]{:S(2)}, u32[]{:S(2)}) collective-permute-start(f32[66,1]{1,0:T(8,128)S(1)} %get-tuple-element.186), channel_id=1, source_target_pairs={{1,0},{2,1},{3,2},{4,3},{5,4},{6,5},{7,6},{9,8},{10,9},{11,10},{12... | collective-permute-start | bytes 800 | tf_op jit(solution)/shard_map/ppermute | solution.py:17
  68.2 9.8 %collective-permute-start.9 = (f32[1,512]{1,0:T(1,128)S(1)}, f32[1,512]{1,0:T(1,128)S(1)}, u32[]{:S(2)}, u32[]{:S(2)}) collective-permute-start(f32[1,512]{1,0:T(1,128)S(1)} %get-tuple-element.234), channel_id=1, source_target_pairs={{8,0},{16,8},{24,16},{9,1},{17,9},{25,17},{10,2},{18,10},{26,18},{... | collective-permute-start | bytes 6152 | tf_op jit(solution)/shard_map/ppermute | solution.py:17
  70.3 7.6 %collective-permute-start.8 = (f32[1,512]{1,0:T(1,128)S(1)}, f32[1,512]{1,0:T(1,128)S(1)}, u32[]{:S(2)}, u32[]{:S(2)}) collective-permute-start(f32[1,512]{1,0:T(1,128)S(1)} %get-tuple-element.233), channel_id=1, source_target_pairs={{0,8},{8,16},{16,24},{1,9},{9,17},{17,25},{2,10},{10,18},{18,26},{... | collective-permute-start | bytes 6152 | tf_op jit(solution)/shard_map/ppermute | solution.py:14
  74.5 11.9 %collective-permute-start.21 = (f32[1,512]{1,0:T(1,128)S(1)}, f32[1,512]{1,0:T(1,128)S(1)}, u32[]{:S(2)}, u32[]{:S(2)}) collective-permute-start(f32[1,512]{1,0:T(1,128)S(1)} %get-tuple-element.228), channel_id=1, source_target_pairs={{8,0},{16,8},{24,16},{9,1},{17,9},{25,17},{10,2},{18,10},{26,18},{... | collective-permute-start | bytes 6152 | tf_op jit(solution)/shard_map/ppermute | solution.py:17
  76.6 9.8 %collective-permute-start.20 = (f32[1,512]{1,0:T(1,128)S(1)}, f32[1,512]{1,0:T(1,128)S(1)}, u32[]{:S(2)}, u32[]{:S(2)}) collective-permute-start(f32[1,512]{1,0:T(1,128)S(1)} %get-tuple-element.227), channel_id=1, source_target_pairs={{0,8},{8,16},{16,24},{1,9},{9,17},{17,25},{2,10},{10,18},{18,26},{... | collective-permute-start | bytes 6152 | tf_op jit(solution)/shard_map/ppermute | solution.py:14
  78.0 16.2 %collective-permute-start.10 = (f32[66,1]{1,0:T(8,128)S(1)}, f32[66,1]{1,0:T(8,128)S(1)}, u32[]{:S(2)}, u32[]{:S(2)}) collective-permute-start(f32[66,1]{1,0:T(8,128)S(1)} %get-tuple-element.193), channel_id=1, source_target_pairs={{0,1},{1,2},{2,3},{3,4},{4,5},{5,6},{6,7},{8,9},{9,10},{10,11},{11... | collective-permute-start | bytes 800 | tf_op jit(solution)/shard_map/ppermute | solution.py:14
  84.5 9.7 %collective-permute-start.11 = (f32[66,1]{1,0:T(8,128)S(1)}, f32[66,1]{1,0:T(8,128)S(1)}, u32[]{:S(2)}, u32[]{:S(2)}) collective-permute-start(f32[66,1]{1,0:T(8,128)S(1)} %get-tuple-element.194), channel_id=1, source_target_pairs={{1,0},{2,1},{3,2},{4,3},{5,4},{6,5},{7,6},{9,8},{10,9},{11,10},{12... | collective-permute-start | bytes 800 | tf_op jit(solution)/shard_map/ppermute | solution.py:17
  86.5 7.8 %collective-permute-start.22 = (f32[66,1]{1,0:T(8,128)S(1)}, f32[66,1]{1,0:T(8,128)S(1)}, u32[]{:S(2)}, u32[]{:S(2)}) collective-permute-start(f32[66,1]{1,0:T(8,128)S(1)} %get-tuple-element.181), channel_id=1, source_target_pairs={{0,1},{1,2},{2,3},{3,4},{4,5},{5,6},{6,7},{8,9},{9,10},{10,11},{11... | collective-permute-start | bytes 800 | tf_op jit(solution)/shard_map/ppermute | solution.py:14
  92.3 7.4 %collective-permute-start.23 = (f32[66,1]{1,0:T(8,128)S(1)}, f32[66,1]{1,0:T(8,128)S(1)}, u32[]{:S(2)}, u32[]{:S(2)}) collective-permute-start(f32[66,1]{1,0:T(8,128)S(1)} %get-tuple-element.182), channel_id=1, source_target_pairs={{1,0},{2,1},{3,2},{4,3},{5,4},{6,5},{7,6},{9,8},{10,9},{11,10},{12... | collective-permute-start | bytes 800 | tf_op jit(solution)/shard_map/ppermute | solution.py:17
  120.7 7.4 %collective-permute-start.28 = (f32[66,1]{1,0:T(8,128)S(1)}, f32[66,1]{1,0:T(8,128)S(1)}, u32[]{:S(2)}, u32[]{:S(2)}) collective-permute-start(f32[66,1]{1,0:T(8,128)S(1)} %get-tuple-element.178), channel_id=1, source_target_pairs={{1,0},{2,1},{3,2},{4,3},{5,4},{6,5},{7,6},{9,8},{10,9},{11,10},{12... | collective-permute-start | bytes 800 | tf_op jit(solution)/shard_map/ppermute | solution.py:17
  138.4 7.4 %collective-permute-start.32 = (f32[66,1]{1,0:T(8,128)S(1)}, f32[66,1]{1,0:T(8,128)S(1)}, u32[]{:S(2)}, u32[]{:S(2)}) collective-permute-start(f32[66,1]{1,0:T(8,128)S(1)} %get-tuple-element.174), channel_id=1, source_target_pairs={{1,0},{2,1},{3,2},{4,3},{5,4},{6,5},{7,6},{9,8},{10,9},{11,10},{12... | collective-permute-start | bytes 800 | tf_op jit(solution)/shard_map/ppermute | solution.py:17
  163.8 7.5 %collective-permute-start.37 = (f32[66,1]{1,0:T(8,128)S(1)}, f32[66,1]{1,0:T(8,128)S(1)}, u32[]{:S(2)}, u32[]{:S(2)}) collective-permute-start(f32[66,1]{1,0:T(8,128)S(1)} %get-tuple-element.170), channel_id=1, source_target_pairs={{1,0},{2,1},{3,2},{4,3},{5,4},{6,5},{7,6},{9,8},{10,9},{11,10},{12... | collective-permute-start | bytes 800 | tf_op jit(solution)/shard_map/ppermute | solution.py:17
  181.4 7.5 %collective-permute-start.41 = (f32[66,1]{1,0:T(8,128)S(1)}, f32[66,1]{1,0:T(8,128)S(1)}, u32[]{:S(2)}, u32[]{:S(2)}) collective-permute-start(f32[66,1]{1,0:T(8,128)S(1)} %get-tuple-element.166), channel_id=1, source_target_pairs={{1,0},{2,1},{3,2},{4,3},{5,4},{6,5},{7,6},{9,8},{10,9},{11,10},{12... | collective-permute-start | bytes 800 | tf_op jit(solution)/shard_map/ppermute | solution.py:17
  (66 other events, 361.4 us)
where the time goes:
time: 408 us; the launch traced here: 405 us
  starting transfers between devices  215 us (53%)
  waiting for transfers between devices  169 us (41%)
  other arithmetic  19.4 us (5%)
    ppermute x40, starting transfers between devices, with_halo(): lax.ppermute(lax.slice_in_dim(block, block.shape[dim] - width, None, axis...  117 us
    ppermute x40, waiting for transfers between devices, with_halo(): lax.ppermute(lax.slice_in_dim(block, 0, width, axis=dim), axis, backward)  90.6 us
    ppermute x40, starting transfers between devices, with_halo(): lax.ppermute(lax.slice_in_dim(block, 0, width, axis=dim), axis, backward)  81.4 us
    ppermute x40, waiting for transfers between devices, with_halo(): lax.ppermute(lax.slice_in_dim(block, block.shape[dim] - width, None, axis...  48.4 us
    ppermute x7, waiting for transfers between devices, shifted(): lax.ppermute(value, axis, [(source, source + steps) for source in range(f...  30.1 us
    ppermute x7, starting transfers between devices, shifted(): lax.ppermute(value, axis, [(source, source + steps) for source in range(f...  16.2 us
  transfers between devices with their start and end apart: 87, of which 42 were waited for; matrix products, arithmetic and copies ran while one was open for 1% of the time, Pallas kernels for 0%

commit v1 on v0

v1 whole, which is shorter than its diff:
```python
import functools

import jax
import jax.numpy as jnp
from jax import lax
from jax.experimental import pallas as pl
from jax.experimental.pallas import tpu as pltpu
from jax.sharding import PartitionSpec as P

MESH = pl.DeviceIdType.MESH
NT = 8
TR = 64
TC = 512
LT = 128
HB = 24
WR = TR + 2 * HB
DIRS = [(-1, -1), (-1, 0), (-1, 1), (0, -1), (0, 1), (1, -1), (1, 0), (1, 1)]
ROWS = [(0, 0, 0, 112), (1, 4, 8, 96), (5, 7, 16, 80)]


def row_span(section):
    for first, last, start, rows in ROWS:
        if first <= section <= last:
            return start, rows


def roll(value, shift, axis):
    return pltpu.roll(value, shift % value.shape[axis], axis)


def kernel(
    gxn, gyn, u_ref, cond_ref, vel_ref, out_ref,
    ubuf, wbuf, xbuf, main, other, cwin, cedge, coef, fsend, frecv,
    load_sem, su, ru, sc, rc, sx, rx, sf, rf,
):
    ta = lax.axis_index("ta")
    gx = lax.axis_index("gx")
    gy = lax.axis_index("gy")
    even = lax.rem(ta, 2) == 0
    tile_m = ta // 2
    tile_o = lax.rem(tile_m + jnp.where(even, 3, 1), 4)

    def has(dx, dy):
        x, y = gx + dx, gy + dy
        return (x >= 0) & (x < gxn) & (y >= 0) & (y < gyn)

    lanes_m = pl.ds(pl.multiple_of(tile_m * LT, LT), LT)
    lanes_o = pl.ds(pl.multiple_of(tile_o * LT, LT), LT)
    loads = [
        pltpu.make_async_copy(u_ref.at[0], ubuf.at[pl.ds(HB, TR), pl.ds(0, TC)], load_sem.at[0]),
        pltpu.make_async_copy(cond_ref.at[:, lanes_m], main.at[0], load_sem.at[1]),
        pltpu.make_async_copy(cond_ref.at[:, lanes_o], other.at[0], load_sem.at[2]),
        pltpu.make_async_copy(vel_ref.at[:, :, lanes_m], main.at[pl.ds(1, 2)], load_sem.at[3]),
        pltpu.make_async_copy(vel_ref.at[:, :, lanes_o], other.at[pl.ds(1, 2)], load_sem.at[4]),
    ]
    for load in loads:
        load.start()

    ubuf[0:HB, :] = jnp.zeros((HB, 6 * LT), jnp.float32)
    ubuf[HB + TR : WR, :] = jnp.zeros((HB, 6 * LT), jnp.float32)
    ubuf[HB : HB + TR, TC:] = jnp.zeros((TR, 2 * LT), jnp.float32)
    cwin[:, 0:HB, :] = jnp.zeros((3, HB, LT), jnp.float32)
    cwin[:, HB + TR : WR, :] = jnp.zeros((3, HB, LT), jnp.float32)
    cedge[...] = jnp.zeros((3, WR, LT), jnp.float32)

    barrier = pltpu.get_barrier_semaphore()
    count = NT - 1
    for dx, dy in DIRS:
        near = has(dx, dy)
        count = count + near.astype(jnp.int32)

        @pl.when(near)
        def _():
            pl.semaphore_signal(barrier, inc=1, device_id=(ta, gx + dx, gy + dy), device_id_type=MESH)

    for step in range(1, NT):
        pl.semaphore_signal(
            barrier, inc=1, device_id=(lax.rem(ta + step, NT), gx, gy), device_id_type=MESH
        )
    for load in loads:
        load.wait()

    lane = lax.broadcasted_iota(jnp.int32, (TR, LT), 1)
    use_m = jnp.where(even, lane, LT - 1 - lane) < 96
    for part in range(3):
        cwin[part, HB : HB + TR, :] = jnp.where(use_m, main[part], other[part])
    pl.semaphore_wait(barrier, count)

    src_rows = {-1: pl.ds(0, HB), 0: pl.ds(0, TR), 1: pl.ds(TR - HB, HB)}
    dst_rows = {-1: pl.ds(HB + TR, HB), 0: pl.ds(HB, TR), 1: pl.ds(0, HB)}
    src_cols = {-1: pl.ds(0, LT), 0: pl.ds(0, TC), 1: pl.ds(TC - LT, LT)}
    dst_cols = {-1: pl.ds(TC, LT), 0: pl.ds(0, TC), 1: pl.ds(TC + LT, LT)}
    own_rows = {-1: pl.ds(HB, HB), 0: pl.ds(HB, TR), 1: pl.ds(TR, HB)}

    def state_copy(at):
        dx, dy = DIRS[at]
        return pltpu.make_async_remote_copy(
            src_ref=ubuf.at[own_rows[dx], src_cols[dy]],
            dst_ref=ubuf.at[dst_rows[dx], dst_cols[dy]],
            send_sem=su.at[at],
            recv_sem=ru.at[at],
            device_id=(ta, gx + dx, gy + dy),
            device_id_type=MESH,
        )

    def coef_copy(at):
        dx, dy = DIRS[at]
        if dy == 0:
            src, dst = cwin.at[:, own_rows[dx], :], cwin.at[:, dst_rows[dx], :]
        else:
            src, dst = other.at[:, src_rows[dx], :], cedge.at[:, dst_rows[dx], :]
        return pltpu.make_async_remote_copy(
            src_ref=src,
            dst_ref=dst,
            send_sem=sc.at[at],
            recv_sem=rc.at[at],
            device_id=(ta, gx + dx, gy + dy),
            device_id_type=MESH,
        )

    def coef_goes(dy):
        return {-1: ta == NT - 1, 0: ta >= 0, 1: ta == 0}[dy]

    for at, (dx, dy) in enumerate(DIRS):

        @pl.when(has(dx, dy))
        def _():
            state_copy(at).start()

    for at, (dx, dy) in enumerate(DIRS):

        @pl.when(has(dx, dy) & coef_goes(dy))
        def _():
            coef_copy(at).start()

    for at, (dx, dy) in enumerate(DIRS):

        @pl.when(has(-dx, -dy))
        def _():
            state_copy(at).wait_recv()

    wlane = lax.broadcasted_iota(jnp.int32, (WR, LT), 1)
    for owner in range(NT):
        tile = owner // 2
        if owner % 2 == 0:
            mate = tile - 1 if tile else 5
            keep = wlane < 96
        else:
            mate = tile + 1
            keep = wlane >= 32
        window = jnp.where(
            keep, ubuf[:, tile * LT : (tile + 1) * LT], ubuf[:, mate * LT : (mate + 1) * LT]
        )
        wbuf[owner] = window

    def window_copy(owner, span):
        start, rows = span
        return pltpu.make_async_remote_copy(
            src_ref=wbuf.at[owner, pl.ds(start, rows)],
            dst_ref=xbuf.at[ta, pl.ds(start, rows)],
            send_sem=sx.at[owner],
            recv_sem=rx.at[ta],
            device_id=(owner, gx, gy),
            device_id_type=MESH,
        )

    for first, last, start, rows in ROWS:

        @pl.when((ta >= first) & (ta <= last))
        def _():
            for step in range(1, NT):
                window_copy(lax.rem(ta + step, NT), (start, rows)).start()

    xbuf[ta] = wbuf[ta]

    for at, (dx, dy) in enumerate(DIRS):

        @pl.when(has(-dx, -dy) & coef_goes(dy))
        def _():
            coef_copy(at).wait_recv()

    row = lax.broadcasted_iota(jnp.int32, (WR, LT), 0)
    keep_m = jnp.where(even, wlane, LT - 1 - wlane) < 96
    take_edge = jnp.logical_not(keep_m) & ((ta == 0) | (ta == NT - 1))

    def mean(part):
        value = jnp.where(take_edge, cedge[part], cwin[part])
        value = value + roll(value, -1, 1)
        return value + roll(value, -1, 0)

    stiff = mean(0) * (0.25 * 0.1 / 6.0)
    vx = mean(1) * (0.25 * 0.1 / 8.0)
    vy = mean(2) * (0.25 * 0.1 / 8.0)
    gam = vx + vy
    kap = vx - vy
    column = (
        gy * TC + ta * 64 + jnp.where(
            even,
            jnp.where(wlane < 96, wlane, wlane - LT),
            jnp.where(wlane < 32, wlane + 64, wlane - 64),
        )
    )
    line = gx * TR + row - HB
    inside = (column >= 0) & (column < gyn * TC) & (line >= 0) & (line < gxn * TR)

    def put(slot, shift, value):
        coef[slot] = roll(jnp.where(inside, value, 0.0), shift, 0)

    def before(value):
        return roll(value, 1, 0)

    def left(value):
        return roll(value, 1, 1)

    put(0, 0, (4.0 * stiff - gam) + before(4.0 * stiff + kap) + left(4.0 * stiff - kap + before(4.0 * stiff + gam)))
    put(1, 0, (-stiff - kap) + before(gam - stiff))
    put(2, 0, left((-stiff - gam) + before(kap - stiff)))
    put(3, 1, (kap - stiff) + left(gam - stiff))
    put(4, 1, gam - 2.0 * stiff)
    put(5, 1, left(kap - 2.0 * stiff))
    put(6, -1, before((-stiff - gam) + left(-stiff - kap)))
    put(7, -1, before(-kap - 2.0 * stiff))
    put(8, -1, left(before(-gam - 2.0 * stiff)))

    def rate(value, span):
        start, rows = span
        high = roll(value, -1, 1)
        low = roll(value, 1, 1)

        def line_sum(slot):
            return (
                coef[slot, start : start + rows] * value
                + coef[slot + 1, start : start + rows] * high
                + coef[slot + 2, start : start + rows] * low
            )

        return line_sum(0) + roll(line_sum(3), -1, 0) + roll(line_sum(6), 1, 0)

    def trim(value, old, new):
        skip = new[0] - old[0]
        return value[skip : skip + new[1]]

    def result_copy(section):
        return pltpu.make_async_remote_copy(
            src_ref=fsend.at[section],
            dst_ref=frecv.at[ta],
            send_sem=sf.at[section],
            recv_sem=rf.at[ta],
            device_id=(section, gx, gy),
            device_id_type=MESH,
        )

    flane = lax.broadcasted_iota(jnp.int32, (TR // 2, LT), 1)
    fmain = jnp.where(even, flane, LT - 1 - flane) < 64
    state, state_span = None, None
    for section in range(NT):
        span = row_span(section)
        start, rows = span

        @pl.when(ta != section)
        def _():
            pltpu.make_async_remote_copy(
                src_ref=wbuf.at[section, pl.ds(start, rows)],
                dst_ref=xbuf.at[section, pl.ds(start, rows)],
                send_sem=sx.at[section],
                recv_sem=rx.at[section],
                device_id=(section, gx, gy),
                device_id_type=MESH,
            ).wait_recv()

        value = xbuf[section, start : start + rows]
        r1 = rate(value, span)
        r2 = rate(r1, span)
        r3 = rate(r2, span)
        r4 = rate(r3, span)
        delta = 0.25 * r4 - r3
        if section == 0:
            state, state_span = value - 2.0 * (r1 - r2) + delta, span
        else:
            now = row_span(section + 1 if section == 4 else section)
            state = trim(state, state_span, now)
            first = rate(state, now)
            second = rate(first, now)
            state = state - 2.0 * (first - second) + trim(delta, span, now)
            state_span = now
        tile = trim(state, state_span, (HB, TR))
        folded = jnp.where(fmain, tile[: TR // 2], roll(tile[TR // 2 :], 64, 1))
        fsend[section] = folded

        @pl.when(ta != section)
        def _():
            result_copy(section).start()

    frecv[ta] = fsend[ta]

    for step in range(1, NT):
        peer = lax.rem(ta + step, NT)
        pltpu.make_async_remote_copy(
            src_ref=fsend.at[peer],
            dst_ref=frecv.at[peer],
            send_sem=sf.at[peer],
            recv_sem=rf.at[peer],
            device_id=(peer, gx, gy),
            device_id_type=MESH,
        ).wait_recv()

    for tile in range(4):
        lower, upper = frecv[2 * tile], frecv[2 * tile + 1]
        lanes = slice(tile * LT, (tile + 1) * LT)
        out_ref[0, : TR // 2, lanes] = jnp.where(flane < 64, lower, upper)
        out_ref[0, TR // 2 :, lanes] = roll(jnp.where(flane < 64, upper, lower), 64, 1)

    for at, (dx, dy) in enumerate(DIRS):

        @pl.when(has(dx, dy))
        def _():
            state_copy(at).wait_send()

        @pl.when(has(dx, dy) & coef_goes(dy))
        def _():
            coef_copy(at).wait_send()

    for first, last, start, rows in ROWS:

        @pl.when((ta >= first) & (ta <= last))
        def _():
            for step in range(1, NT):
                window_copy(lax.rem(ta + step, NT), (start, rows)).wait_send()

    for step in range(1, NT):
        result_copy(lax.rem(ta + step, NT)).wait_send()


def solution(mesh):
    gxn, gyn = mesh.shape["gx"], mesh.shape["gy"]

    def local(start_states, conduct, velocity):
        return pl.pallas_call(
            functools.partial(kernel, gxn, gyn),
            out_shape=jax.ShapeDtypeStruct((1, TR, TC), jnp.float32),
            in_specs=[pl.BlockSpec(memory_space=pl.ANY)] * 3,
            out_specs=pl.BlockSpec(memory_space=pltpu.VMEM),
            scratch_shapes=[
                pltpu.VMEM((WR, 6 * LT), jnp.float32),
                pltpu.VMEM((NT, WR, LT), jnp.float32),
                pltpu.VMEM((NT, WR, LT), jnp.float32),
                pltpu.VMEM((3, TR, LT), jnp.float32),
                pltpu.VMEM((3, TR, LT), jnp.float32),
                pltpu.VMEM((3, WR, LT), jnp.float32),
                pltpu.VMEM((3, WR, LT), jnp.float32),
                pltpu.VMEM((9, WR, LT), jnp.float32),
                pltpu.VMEM((NT, TR // 2, LT), jnp.float32),
                pltpu.VMEM((NT, TR // 2, LT), jnp.float32),
                pltpu.SemaphoreType.DMA((5,)),
            ]
            + [pltpu.SemaphoreType.DMA((8,))] * 8,
            compiler_params=pltpu.CompilerParams(
                collective_id=0, has_side_effects=True, vmem_limit_bytes=32 * 1024 * 1024
            ),
        )(start_states, conduct, velocity)

    in_specs = (P("ta", "gx", "gy"), P("gx", "gy"), P(None, "gx", "gy"))
    return jax.shard_map(
        local, mesh=mesh, in_specs=in_specs, out_specs=P("ta", "gx", "gy"), check_vma=False
    )
```

time: 408 us -> 25.4 us (0.06)
  the two profiles are of different devices: /device:TPU:79 before, /device:TPU:89 now
where the time goes in v1:
time: 25.4 us; the launch traced here: 25.3 us
  Pallas kernels  21.9 us (86%)
  local copies, waits for them, and re-layouts  3.41 us (13%)
    pallas_call x1, Pallas kernels, local(): pl.pallas_call(functools.partial(kernel, gxn, gyn), out_shape=jax.ShapeDt...  21.9 us
    unnamed x7, local copies, waits for them, and re-layouts  3.41 us

profile of v1, /device:TPU:89, one launch (start us, length us, event | category | flops | bytes accessed | tf_op | source)
XLA Modules:
  0.0 25.3 jit_solution(16031913921470016848)
XLA Ops:
  0.0 0.0 copy-start
  0.0 0.9 %copy-done = f32[2,64,512]{2,1,0:T(8,128)S(1)} copy-done((f32[2,64,512]{2,1,0:T(8,128)S(1)}, f32[2,64,512]{2,1,0:T(8,128)}, u32[]{:S(2)}) %copy-start) | copy-done | bytes 262168
  1.0 0.0 copy-start.1
  1.0 0.9 %copy-done.1 = f32[1,64,512]{2,1,0:T(8,128)S(1)} copy-done((f32[1,64,512]{2,1,0:T(8,128)S(1)}, f32[1,64,512]{2,1,0:T(8,128)}, u32[]{:S(2)}) %copy-start.1) | copy-done | bytes 131096
  1.9 0.0 copy-start.2
  1.9 0.9 %copy-done.2 = f32[64,512]{1,0:T(8,128)S(1)} copy-done((f32[64,512]{1,0:T(8,128)S(1)}, f32[64,512]{1,0:T(8,128)}, u32[]{:S(2)}) %copy-start.2) | copy-done | bytes 131096
  2.8 21.9 %shard_map.37 = f32[1,64,512]{2,1,0:T(8,128)S(1)} custom-call(f32[1,64,512]{2,1,0:T(8,128)S(1)} %copy-done.1, f32[64,512]{1,0:T(8,128)S(1)} %copy-done.2, f32[2,64,512]{2,1,0:T(8,128)S(1)} %copy-done), custom_call_target="tpu_custom_call" | custom-call | tf_op jit(solution)/shard_map/pallas_call | solution.py:338
  24.6 0.7 %copy.5 = f32[1,64,512]{2,1,0:T(8,128)} copy(f32[1,64,512]{2,1,0:T(8,128)S(1)} %shard_map.37) | data formatting | bytes 262144
Async XLA Ops:
  0.0 0.9 %copy-start = (f32[2,64,512]{2,1,0:T(8,128)S(1)}, f32[2,64,512]{2,1,0:T(8,128)}, u32[]{:S(2)}) copy-start(f32[2,64,512]{2,1,0:T(8,128)} %vel_ref.1) | copy-start | bytes 786436
  1.0 0.9 %copy-start.1 = (f32[1,64,512]{2,1,0:T(8,128)S(1)}, f32[1,64,512]{2,1,0:T(8,128)}, u32[]{:S(2)}) copy-start(f32[1,64,512]{2,1,0:T(8,128)} %u_ref.1) | copy-start | bytes 393220
  1.9 0.9 %copy-start.2 = (f32[64,512]{1,0:T(8,128)S(1)}, f32[64,512]{1,0:T(8,128)}, u32[]{:S(2)}) copy-start(f32[64,512]{1,0:T(8,128)} %cond_ref.1) | copy-start | bytes 393220

commit v2 on v1

--- a/solution.py
+++ b/solution.py
@@ -355,7 +355,7 @@
             ]
             + [pltpu.SemaphoreType.DMA((8,))] * 8,
             compiler_params=pltpu.CompilerParams(
-                collective_id=0, has_side_effects=True, vmem_limit_bytes=32 * 1024 * 1024
+                collective_id=0, has_side_effects=True
             ),
         )(start_states, conduct, velocity)
 

time: 25.4 us -> 24.1 us (0.949)
  local copies, waits for them, and re-layouts: 3.41 us -> 1.57 us
  Pallas kernels: 21.9 us -> 22.5 us
    unnamed x7 -> x1, local copies, waits for them, and re-layouts: 3.41 us -> 1.57 us
    pallas_call x1, Pallas kernels: 21.9 us -> 22.5 us  [local(): pl.pallas_call(functools.partial(kernel, gxn, gyn), out_shape=jax.ShapeDt...]
where the time goes in v2:
time: 24.1 us; the launch traced here: 24 us
  Pallas kernels  22.5 us (93%)
  local copies, waits for them, and re-layouts  1.57 us (7%)
    pallas_call x1, Pallas kernels, local(): pl.pallas_call(functools.partial(kernel, gxn, gyn), out_shape=jax.ShapeDt...  22.5 us
    unnamed x1, local copies, waits for them, and re-layouts  1.57 us

profile of v2, /device:TPU:89, one launch (start us, length us, event | category | flops | bytes accessed | tf_op | source)
XLA Modules:
  0.0 24.0 jit_solution(154917291652717058)
XLA Ops:
  0.0 22.5 %shard_map.37 = f32[1,64,512]{2,1,0:T(8,128)} custom-call(f32[1,64,512]{2,1,0:T(8,128)} %u_ref.1, f32[64,512]{1,0:T(8,128)} %cond_ref.1, f32[2,64,512]{2,1,0:T(8,128)} %vel_ref.1), custom_call_target="tpu_custom_call" | custom-call | tf_op jit(solution)/shard_map/pallas_call | solution.py:338
  22.5 1.6 %copy.5 = f32[1,64,512]{2,1,0:T(8,128)} copy(f32[1,64,512]{2,1,0:T(8,128)} %shard_map.37) | data formatting | bytes 262144

commit v3 on v2

v3 whole, which is shorter than its diff:
```python
import functools

import jax
import jax.numpy as jnp
from jax import lax
from jax.experimental import pallas as pl
from jax.experimental.pallas import tpu as pltpu
from jax.sharding import PartitionSpec as P

MESH = pl.DeviceIdType.MESH
NT = 8
TR = 64
TC = 512
LT = 128
HB = 24
WR = TR + 2 * HB
ER = 32
ROWS = [(0, 0, 0, 112), (1, 4, 8, 96), (5, 7, 16, 80)]
SPANS = [(0, 112), (8, 96), (8, 96), (8, 96), (16, 80), (16, 80), (16, 80), (16, 80)]
EDGE = {1: (0, 8), 0: (8, 16), -1: (24, 8)}


def row_span(section):
    for first, last, start, rows in ROWS:
        if first <= section <= last:
            return start, rows


def roll(value, shift, axis):
    return pltpu.roll(value, shift % value.shape[axis], axis)


def fold(read, base):
    lane = lax.broadcasted_iota(jnp.int32, (8, LT), 1)
    parts = []
    for start, groups in ((40, 3), (0, 4), (32, 4), (0, 3)):
        value = roll(read(start), base, 1)
        for group in range(1, groups):
            moved = roll(read(start + 8 * group), base + 32 * group, 1)
            value = jnp.where(lane < 32 * group, value, moved)
        parts.append(value)
    return parts


def unfold(read, base):
    for start, groups, first in ((0, 3, 0), (8, 4, 3), (16, 4, 7), (24, 3, 11)):
        value = read(start)
        for group in range(groups):
            yield first + group, roll(value, base - 32 * group, 1)


def kernel(
    gxn, gyn, u_ref, cond_ref, vel_ref, out_ref,
    ubuf, wbuf, xbuf, ebuf, xedge, main, other, cwin, cfull, cfold, cedge, coef, fsend, frecv,
    load_sem, s_main, r_main, s_strip, r_strip, s_edge, r_edge, sc, rc, sf, rf,
):
    ta = lax.axis_index("ta")
    gx = lax.axis_index("gx")
    gy = lax.axis_index("gy")
    even = lax.rem(ta, 2) == 0
    tile_m = ta // 2
    tile_o = lax.rem(tile_m + jnp.where(even, 3, 1), 4)

    def has(dx, dy):
        x, y = gx + dx, gy + dy
        return (x >= 0) & (x < gxn) & (y >= 0) & (y < gyn)

    def ring(step):
        return lax.rem(ta + step, NT)

    lanes_m = pl.ds(pl.multiple_of(tile_m * LT, LT), LT)
    lanes_o = pl.ds(pl.multiple_of(tile_o * LT, LT), LT)
    loads = [
        pltpu.make_async_copy(u_ref.at[0], ubuf, load_sem.at[0]),
        pltpu.make_async_copy(cond_ref.at[:, lanes_m], main.at[0], load_sem.at[1]),
        pltpu.make_async_copy(cond_ref.at[:, lanes_o], other.at[0], load_sem.at[2]),
        pltpu.make_async_copy(vel_ref.at[:, :, lanes_m], main.at[pl.ds(1, 2)], load_sem.at[3]),
        pltpu.make_async_copy(vel_ref.at[:, :, lanes_o], other.at[pl.ds(1, 2)], load_sem.at[4]),
    ]
    for load in loads:
        load.start()

    xbuf[:, 0:HB, :] = jnp.zeros((NT, HB, LT), jnp.float32)
    xbuf[:, HB + TR : WR, :] = jnp.zeros((NT, HB, LT), jnp.float32)
    xedge[...] = jnp.zeros((NT, ER, LT), jnp.float32)
    cwin[:, 0:HB, :] = jnp.zeros((3, HB, LT), jnp.float32)
    cwin[:, HB + TR : WR, :] = jnp.zeros((3, HB, LT), jnp.float32)
    cedge[...] = jnp.zeros((3, ER, LT), jnp.float32)

    barrier = pltpu.get_barrier_semaphore()

    def greet(section, dx, dy):
        pl.semaphore_signal(
            barrier, inc=1, device_id=(section, gx + dx, gy + dy), device_id_type=MESH
        )

    for dx in (-1, 1):

        @pl.when(has(dx, 0))
        def _():
            for step in range(NT):
                greet(ring(step), dx, 0)

    for owner, dy in ((0, -1), (NT - 1, 1)):
        for dx in (-1, 0, 1):

            @pl.when((ta == owner) & has(dx, dy))
            def _():
                for step in range(NT):
                    greet(ring(step), dx, dy)

    for step in range(1, NT):
        greet(ring(step), 0, 0)

    count = NT - 1
    for dx in (-1, 1):
        count = count + NT * has(dx, 0).astype(jnp.int32)
    for dy in (-1, 1):
        for dx in (-1, 0, 1):
            count = count + has(dx, dy).astype(jnp.int32)

    for load in loads:
        load.wait()

    lane = lax.broadcasted_iota(jnp.int32, (TR, LT), 1)
    for owner in range(NT):
        tile = owner // 2
        if owner % 2 == 0:
            mate, keep = (tile + 3) % 4, lane < 96
        else:
            mate, keep = (tile + 1) % 4, lane >= 32
        wbuf[owner] = jnp.where(
            keep, ubuf[:, tile * LT : (tile + 1) * LT], ubuf[:, mate * LT : (mate + 1) * LT]
        )
    for slot, (first, base) in enumerate(((3 * LT, 32), (0, 0))):
        for at, part in enumerate(fold(lambda start: ubuf[start : start + 8, first : first + LT], base)):
            ebuf[slot, 8 * at : 8 * at + 8] = part
    use_m = jnp.where(even, lane, LT - 1 - lane) < 96
    for part in range(3):
        cwin[part, HB : HB + TR, :] = jnp.where(use_m, main[part], other[part])
    for owner, base in ((0, 32), (NT - 1, 0)):

        @pl.when(ta == owner)
        def _():
            for part in range(3):
                for at, value in enumerate(fold(lambda start: other[part, start : start + 8], base)):
                    cfold[part, 8 * at : 8 * at + 8] = value

    xbuf[ta, HB : HB + TR] = wbuf[ta]
    pl.semaphore_wait(barrier, count)

    def main_copy(owner, section):
        return pltpu.make_async_remote_copy(
            src_ref=wbuf.at[owner],
            dst_ref=xbuf.at[section, pl.ds(HB, TR)],
            send_sem=s_main.at[owner],
            recv_sem=r_main.at[section],
            device_id=(owner, gx, gy),
            device_id_type=MESH,
        )

    def strip_copy(owner, section, dx, rows, here=False):
        if dx < 0:
            src, dst = pl.ds(0, rows), pl.ds(HB + TR, rows)
        else:
            src, dst = pl.ds(TR - rows, rows), pl.ds(HB - rows, rows)
        side = (dx + 1) // 2
        return pltpu.make_async_remote_copy(
            src_ref=wbuf.at[owner, src],
            dst_ref=xbuf.at[section, dst],
            send_sem=s_strip.at[NT * side + owner],
            recv_sem=r_strip.at[NT * side + section],
            device_id=(ta, gx, gy) if here else (owner, gx + dx, gy),
            device_id_type=MESH,
        )

    def edge_copy(section, dx, dy, here=False):
        slot, owner = (0, 0) if dy > 0 else (1, NT - 1)
        start, rows = EDGE[dx]
        return pltpu.make_async_remote_copy(
            src_ref=ebuf.at[slot, pl.ds(start, rows)],
            dst_ref=xedge.at[section, pl.ds(start, rows)],
            send_sem=s_edge.at[3 * slot + dx + 1],
            recv_sem=r_edge.at[3 * section + dx + 1],
            device_id=(ta, gx, gy) if here else (ring(lax.rem(owner + NT - ta, NT)), gx + dx, gy + dy),
            device_id_type=MESH,
        )

    def coef_copy(dx, dy, here=False):
        if dy == 0:
            if dx < 0:
                src, dst = pl.ds(HB, HB), pl.ds(HB + TR, HB)
            else:
                src, dst = pl.ds(TR, HB), pl.ds(0, HB)
            src, dst = cwin.at[:, src, :], cwin.at[:, dst, :]
        else:
            place = pl.ds(*EDGE[dx])
            src, dst = cfold.at[:, place, :], cedge.at[:, place, :]
        at = 3 * (1 if dy else 0) + dx + 1
        return pltpu.make_async_remote_copy(
            src_ref=src,
            dst_ref=dst,
            send_sem=sc.at[at],
            recv_sem=rc.at[at],
            device_id=(ta, gx, gy) if here else (ta, gx + dx, gy + dy),
            device_id_type=MESH,
        )

    coef_dirs = [(-1, 0, None), (1, 0, None)]
    coef_dirs += [(dx, 1, 0) for dx in (-1, 0, 1)] + [(dx, -1, NT - 1) for dx in (-1, 0, 1)]

    def sends(act):
        for dx, dy, only in coef_dirs:
            near = has(dx, dy)

            @pl.when(near if only is None else near & (ta == only))
            def _():
                act(coef_copy(dx, dy))

        for first, last, _, rows in ROWS:

            @pl.when((ta >= first) & (ta <= last))
            def _():
                for dx in (-1, 1):

                    @pl.when(has(dx, 0))
                    def _():
                        for step in range(NT):
                            act(strip_copy(ring(step), ta, dx, (rows - TR) // 2))

        for step in range(1, NT):
            act(main_copy(ring(step), ta))
        for dy in (-1, 1):
            for dx in (-1, 0, 1):

                @pl.when(has(dx, dy))
                def _():
                    act(edge_copy(ta, dx, dy))

    sends(lambda copy: copy.start())

    for dx, dy, only in coef_dirs:
        near = has(-dx, -dy)

        @pl.when(near if only is None else near & (ta == only))
        def _():
            coef_copy(dx, dy, True).wait_recv()

    cfull[...] = cwin[...]
    edge_lane = lax.broadcasted_iota(jnp.int32, (8, LT), 1)
    for owner, base in ((0, 96), (NT - 1, 0)):

        @pl.when(ta == owner)
        def _():
            mine = (edge_lane >= base) & (edge_lane < base + 32)
            for part in range(3):
                for at, value in unfold(lambda start: cedge[part, start : start + 8], base):
                    rows = slice(8 * at, 8 * at + 8)
                    cfull[part, rows] = jnp.where(mine, value, cfull[part, rows])

    wlane = lax.broadcasted_iota(jnp.int32, (WR, LT), 1)
    row = lax.broadcasted_iota(jnp.int32, (WR, LT), 0)

    def mean(part):
        value = cfull[part]
        value = value + roll(value, -1, 1)
        return value + roll(value, -1, 0)

    stiff = mean(0) * (0.25 * 0.1 / 6.0)
    vx = mean(1) * (0.25 * 0.1 / 8.0)
    vy = mean(2) * (0.25 * 0.1 / 8.0)
    gam = vx + vy
    kap = vx - vy
    column = (
        gy * TC + ta * 64 + jnp.where(
            even,
            jnp.where(wlane < 96, wlane, wlane - LT),
            jnp.where(wlane < 32, wlane + 64, wlane - 64),
        )
    )
    line = gx * TR + row - HB
    inside = (column >= 0) & (column < gyn * TC) & (line >= 0) & (line < gxn * TR)

    def put(slot, shift, value):
        coef[slot] = roll(jnp.where(inside, value, 0.0), shift, 0)

    def before(value):
        return roll(value, 1, 0)

    def left(value):
        return roll(value, 1, 1)

    put(0, 0, (4.0 * stiff - gam) + before(4.0 * stiff + kap) + left(4.0 * stiff - kap + before(4.0 * stiff + gam)))
    put(1, 0, (-stiff - kap) + before(gam - stiff))
    put(2, 0, left((-stiff - gam) + before(kap - stiff)))
    put(3, 1, (kap - stiff) + left(gam - stiff))
    put(4, 1, gam - 2.0 * stiff)
    put(5, 1, left(kap - 2.0 * stiff))
    put(6, -1, before((-stiff - gam) + left(-stiff - kap)))
    put(7, -1, before(-kap - 2.0 * stiff))
    put(8, -1, left(before(-gam - 2.0 * stiff)))

    def rate(value, span):
        start, rows = span
        high = roll(value, -1, 1)
        low = roll(value, 1, 1)

        def line_sum(slot):
            return (
                coef[slot, start : start + rows] * value
                + coef[slot + 1, start : start + rows] * high
                + coef[slot + 2, start : start + rows] * low
            )

        return line_sum(0) + roll(line_sum(3), -1, 0) + roll(line_sum(6), 1, 0)

    def trim(value, old, new):
        skip = new[0] - old[0]
        return value[skip : skip + new[1]]

    def result_copy(section):
        return pltpu.make_async_remote_copy(
            src_ref=fsend.at[section],
            dst_ref=frecv.at[ta],
            send_sem=sf.at[section],
            recv_sem=rf.at[ta],
            device_id=(section, gx, gy),
            device_id_type=MESH,
        )

    flane = lax.broadcasted_iota(jnp.int32, (TR // 2, LT), 1)
    fmain = jnp.where(even, flane, LT - 1 - flane) < 64
    def arrive(section):
        span = row_span(section)
        start, rows = span
        @pl.when(ta != section)
        def _():
            main_copy(section, section).wait_recv()

        for dx in (-1, 1):

            @pl.when(has(-dx, 0))
            def _():
                strip_copy(section, section, dx, (rows - TR) // 2, True).wait_recv()

        for owner, dy, base in ((0, 1, 96), (NT - 1, -1, 0)):

            @pl.when(ta == owner)
            def _():
                for dx in (-1, 0, 1):

                    @pl.when(has(-dx, -dy))
                    def _():
                        edge_copy(section, dx, dy, True).wait_recv()

                mine = (edge_lane >= base) & (edge_lane < base + 32)
                for at, value in unfold(lambda start: xedge[section, start : start + 8], base):
                    place = slice(8 * at, 8 * at + 8)
                    xbuf[section, place] = jnp.where(mine, value, xbuf[section, place])

        value = xbuf[section, start : start + rows]
        return value, 0.5 * rate(value - 0.25 * rate(value, span), span), span

    def advance(state, state_span, half, half_span, span):
        state = trim(state, state_span, span)
        inner = state - trim(half, half_span, span)
        return state - 2.0 * rate(state - rate(inner, span), span)

    def give(section, state, span):
        tile = trim(state, span, (HB, TR))
        folded = jnp.where(fmain, tile[: TR // 2], roll(tile[TR // 2 :], 64, 1))
        fsend[section] = folded

        @pl.when(ta != section)
        def _():
            result_copy(section).start()

    state, half, span = arrive(0)
    half_span = span
    for section in range(NT):
        after = arrive(section + 1) if section + 1 < NT else None
        now = SPANS[section]
        state = advance(state, span, half, half_span, now)
        span = now
        give(section, state, span)
        if after is not None:
            half, half_span = after[1], after[2]

    frecv[ta] = fsend[ta]

    for step in range(1, NT):
        peer = lax.rem(ta + step, NT)
        pltpu.make_async_remote_copy(
            src_ref=fsend.at[peer],
            dst_ref=frecv.at[peer],
            send_sem=sf.at[peer],
            recv_sem=rf.at[peer],
            device_id=(peer, gx, gy),
            device_id_type=MESH,
        ).wait_recv()

    for tile in range(4):
        lower, upper = frecv[2 * tile], frecv[2 * tile + 1]
        lanes = slice(tile * LT, (tile + 1) * LT)
        out_ref[0, : TR // 2, lanes] = jnp.where(flane < 64, lower, upper)
        out_ref[0, TR // 2 :, lanes] = roll(jnp.where(flane < 64, upper, lower), 64, 1)

    sends(lambda copy: copy.wait_send())
    for step in range(1, NT):
        result_copy(lax.rem(ta + step, NT)).wait_send()


def solution(mesh):
    gxn, gyn = mesh.shape["gx"], mesh.shape["gy"]

    def local(start_states, conduct, velocity):
        return pl.pallas_call(
            functools.partial(kernel, gxn, gyn),
            out_shape=pltpu.VMEM((1, TR, TC), jnp.float32),
            in_specs=[pl.BlockSpec(memory_space=pl.ANY)] * 3,
            out_specs=pl.BlockSpec(memory_space=pltpu.VMEM),
            scratch_shapes=[
                pltpu.VMEM((TR, TC), jnp.float32),
                pltpu.VMEM((NT, TR, LT), jnp.float32),
                pltpu.VMEM((NT, WR, LT), jnp.float32),
                pltpu.VMEM((2, ER, LT), jnp.float32),
                pltpu.VMEM((NT, ER, LT), jnp.float32),
                pltpu.VMEM((3, TR, LT), jnp.float32),
                pltpu.VMEM((3, TR, LT), jnp.float32),
                pltpu.VMEM((3, WR, LT), jnp.float32),
                pltpu.VMEM((3, WR, LT), jnp.float32),
                pltpu.VMEM((3, ER, LT), jnp.float32),
                pltpu.VMEM((3, ER, LT), jnp.float32),
                pltpu.VMEM((9, WR, LT), jnp.float32),
                pltpu.VMEM((NT, TR // 2, LT), jnp.float32),
                pltpu.VMEM((NT, TR // 2, LT), jnp.float32),
                pltpu.SemaphoreType.DMA((5,)),
                pltpu.SemaphoreType.DMA((NT,)),
                pltpu.SemaphoreType.DMA((NT,)),
                pltpu.SemaphoreType.DMA((2 * NT,)),
                pltpu.SemaphoreType.DMA((2 * NT,)),
                pltpu.SemaphoreType.DMA((6,)),
                pltpu.SemaphoreType.DMA((3 * NT,)),
                pltpu.SemaphoreType.DMA((6,)),
                pltpu.SemaphoreType.DMA((6,)),
                pltpu.SemaphoreType.DMA((NT,)),
                pltpu.SemaphoreType.DMA((NT,)),
            ],
            compiler_params=pltpu.CompilerParams(collective_id=0, has_side_effects=True),
        )(start_states, conduct, velocity)

    in_specs = (P("ta", "gx", "gy"), P("gx", "gy"), P(None, "gx", "gy"))
    return jax.shard_map(
        local, mesh=mesh, in_specs=in_specs, out_specs=P("ta", "gx", "gy"), check_vma=False
    )
```

time: 24.1 us -> 21.8 us (0.905)
  the two profiles are of different devices: /device:TPU:89 before, /device:TPU:1 now
where the time goes in v3:
time: 21.8 us; the launch traced here: 21.7 us
  Pallas kernels  21 us (96%)
  local copies, waits for them, and re-layouts  0.66 us (3%)
    pallas_call x1, Pallas kernels, local(): pl.pallas_call(functools.partial(kernel, gxn, gyn), out_shape=pltpu.VMEM(...  21 us
    unnamed x1, local copies, waits for them, and re-layouts  0.66 us

profile of v3, /device:TPU:1, one launch (start us, length us, event | category | flops | bytes accessed | tf_op | source)
XLA Modules:
  0.0 21.7 jit_solution(9009531506056071435)
XLA Ops:
  0.0 21.0 %shard_map.37 = f32[1,64,512]{2,1,0:T(8,128)S(1)} custom-call(f32[1,64,512]{2,1,0:T(8,128)} %u_ref.1, f32[64,512]{1,0:T(8,128)} %cond_ref.1, f32[2,64,512]{2,1,0:T(8,128)} %vel_ref.1), custom_call_target="tpu_custom_call" | custom-call | tf_op jit(solution)/shard_map/pallas_call | solution.py:417
  21.1 0.7 %copy.5 = f32[1,64,512]{2,1,0:T(8,128)} copy(f32[1,64,512]{2,1,0:T(8,128)S(1)} %shard_map.37) | data formatting | bytes 262144

commit v4 on v3

--- a/solution.py
+++ b/solution.py
@@ -15,15 +15,11 @@
 HB = 24
 WR = TR + 2 * HB
 ER = 32
-ROWS = [(0, 0, 0, 112), (1, 4, 8, 96), (5, 7, 16, 80)]
-SPANS = [(0, 112), (8, 96), (8, 96), (8, 96), (16, 80), (16, 80), (16, 80), (16, 80)]
+ROWS = [(0, 0, 24), (1, 7, 16)]
+FULL = (0, WR)
+SPAN = (8, WR - 16)
+LAST = (16, WR - 32)
 EDGE = {1: (0, 8), 0: (8, 16), -1: (24, 8)}
-
-
-def row_span(section):
-    for first, last, start, rows in ROWS:
-        if first <= section <= last:
-            return start, rows
 
 
 def roll(value, shift, axis):
@@ -51,7 +47,7 @@
 
 def kernel(
     gxn, gyn, u_ref, cond_ref, vel_ref, out_ref,
-    ubuf, wbuf, xbuf, ebuf, xedge, main, other, cwin, cfull, cfold, cedge, coef, fsend, frecv,
+    ubuf, wbuf, xbuf, ebuf, xedge, main, other, cwin, cfull, cfold, cedge, coef, state, half, fsend, frecv,
     load_sem, s_main, r_main, s_strip, r_strip, s_edge, r_edge, sc, rc, sf, rf,
 ):
     ta = lax.axis_index("ta")
@@ -67,6 +63,31 @@
 
     def ring(step):
         return lax.rem(ta + step, NT)
+
+    barrier = pltpu.get_barrier_semaphore()
+
+    def greet(section, dx, dy):
+        pl.semaphore_signal(
+            barrier, inc=1, device_id=(section, gx + dx, gy + dy), device_id_type=MESH
+        )
+
+    for dx in (-1, 1):
+
+        @pl.when(has(dx, 0))
+        def _():
+            for step in range(NT):
+                greet(ring(step), dx, 0)
+
+    for owner, dy in ((0, -1), (NT - 1, 1)):
+        for dx in (-1, 0, 1):
+
+            @pl.when((ta == owner) & has(dx, dy))
+            def _():
+                for step in range(NT):
+                    greet(ring(step), dx, dy)
+
+    for step in range(1, NT):
+        greet(ring(step), 0, 0)
 
     lanes_m = pl.ds(pl.multiple_of(tile_m * LT, LT), LT)
     lanes_o = pl.ds(pl.multiple_of(tile_o * LT, LT), LT)
@@ -80,44 +101,30 @@
     for load in loads:
         load.start()
 
-    xbuf[:, 0:HB, :] = jnp.zeros((NT, HB, LT), jnp.float32)
-    xbuf[:, HB + TR : WR, :] = jnp.zeros((NT, HB, LT), jnp.float32)
-    xedge[...] = jnp.zeros((NT, ER, LT), jnp.float32)
-    cwin[:, 0:HB, :] = jnp.zeros((3, HB, LT), jnp.float32)
-    cwin[:, HB + TR : WR, :] = jnp.zeros((3, HB, LT), jnp.float32)
-    cedge[...] = jnp.zeros((3, ER, LT), jnp.float32)
-
-    barrier = pltpu.get_barrier_semaphore()
-
-    def greet(section, dx, dy):
-        pl.semaphore_signal(
-            barrier, inc=1, device_id=(section, gx + dx, gy + dy), device_id_type=MESH
-        )
-
-    for dx in (-1, 1):
-
-        @pl.when(has(dx, 0))
-        def _():
-            for step in range(NT):
-                greet(ring(step), dx, 0)
-
-    for owner, dy in ((0, -1), (NT - 1, 1)):
-        for dx in (-1, 0, 1):
-
-            @pl.when((ta == owner) & has(dx, dy))
-            def _():
-                for step in range(NT):
-                    greet(ring(step), dx, dy)
-
-    for step in range(1, NT):
-        greet(ring(step), 0, 0)
-
     count = NT - 1
     for dx in (-1, 1):
         count = count + NT * has(dx, 0).astype(jnp.int32)
     for dy in (-1, 1):
         for dx in (-1, 0, 1):
             count = count + has(dx, dy).astype(jnp.int32)
+
+    def clear(ref, planes, start, rows):
+        ref[:, start : start + rows, :] = jnp.zeros((planes, rows, LT), jnp.float32)
+
+    for dx, start in ((1, 0), (-1, HB + TR)):
+
+        @pl.when(jnp.logical_not(has(-dx, 0)))
+        def _():
+            clear(xbuf, NT, start, HB)
+            clear(cwin, 3, start, HB)
+
+    for owner, dy in ((0, 1), (NT - 1, -1)):
+        for dx in (-1, 0, 1):
+
+            @pl.when((ta == owner) & jnp.logical_not(has(-dx, -dy)))
+            def _():
+                clear(xedge, NT, *EDGE[dx])
+                clear(cedge, 3, *EDGE[dx])
 
     for load in loads:
         load.wait()
@@ -210,6 +217,13 @@
     coef_dirs += [(dx, 1, 0) for dx in (-1, 0, 1)] + [(dx, -1, NT - 1) for dx in (-1, 0, 1)]
 
     def sends(act):
+        for dx in (-1, 1, 0):
+            for dy in (-1, 1):
+
+                @pl.when(has(dx, dy))
+                def _():
+                    act(edge_copy(ta, dx, dy))
+
         for dx, dy, only in coef_dirs:
             near = has(dx, dy)
 
@@ -217,7 +231,7 @@
             def _():
                 act(coef_copy(dx, dy))
 
-        for first, last, _, rows in ROWS:
+        for first, last, rows in ROWS:
 
             @pl.when((ta >= first) & (ta <= last))
             def _():
@@ -226,16 +240,10 @@
                     @pl.when(has(dx, 0))
                     def _():
                         for step in range(NT):
-                            act(strip_copy(ring(step), ta, dx, (rows - TR) // 2))
+                            act(strip_copy(ring(step), ta, dx, rows))
 
         for step in range(1, NT):
             act(main_copy(ring(step), ta))
-        for dy in (-1, 1):
-            for dx in (-1, 0, 1):
-
-                @pl.when(has(dx, dy))
-                def _():
-                    act(edge_copy(ta, dx, dy))
 
     sends(lambda copy: copy.start())
 
@@ -330,9 +338,7 @@
 
     flane = lax.broadcasted_iota(jnp.int32, (TR // 2, LT), 1)
     fmain = jnp.where(even, flane, LT - 1 - flane) < 64
-    def arrive(section):
-        span = row_span(section)
-        start, rows = span
+    def arrive(section, halo, span):
         @pl.when(ta != section)
         def _():
             main_copy(section, section).wait_recv()
@@ -341,7 +347,7 @@
 
             @pl.when(has(-dx, 0))
             def _():
-                strip_copy(section, section, dx, (rows - TR) // 2, True).wait_recv()
+                strip_copy(section, section, dx, halo, True).wait_recv()
 
         for owner, dy, base in ((0, 1, 96), (NT - 1, -1, 0)):
 
@@ -355,36 +361,39 @@
 
                 mine = (edge_lane >= base) & (edge_lane < base + 32)
                 for at, value in unfold(lambda start: xedge[section, start : start + 8], base):
-                    place = slice(8 * at, 8 * at + 8)
-                    xbuf[section, place] = jnp.where(mine, value, xbuf[section, place])
-
-        value = xbuf[section, start : start + rows]
-        return value, 0.5 * rate(value - 0.25 * rate(value, span), span), span
-
-    def advance(state, state_span, half, half_span, span):
-        state = trim(state, state_span, span)
-        inner = state - trim(half, half_span, span)
-        return state - 2.0 * rate(state - rate(inner, span), span)
-
-    def give(section, state, span):
-        tile = trim(state, span, (HB, TR))
-        folded = jnp.where(fmain, tile[: TR // 2], roll(tile[TR // 2 :], 64, 1))
-        fsend[section] = folded
+                    if span[0] <= 8 * at < span[0] + span[1]:
+                        place = slice(8 * at, 8 * at + 8)
+                        xbuf[section, place] = jnp.where(mine, value, xbuf[section, place])
+
+        value = xbuf[section, span[0] : span[0] + span[1]]
+        return 0.5 * rate(value - 0.25 * rate(value, span), span)
+
+    def advance(value, half, span):
+        return value - 2.0 * rate(value - rate(value - half, span), span)
+
+    def give(section, value, span):
+        tile = trim(value, span, (HB, TR))
+        fsend[section] = jnp.where(fmain, tile[: TR // 2], roll(tile[TR // 2 :], 64, 1))
 
         @pl.when(ta != section)
         def _():
             result_copy(section).start()
 
-    state, half, span = arrive(0)
-    half_span = span
-    for section in range(NT):
-        after = arrive(section + 1) if section + 1 < NT else None
-        now = SPANS[section]
-        state = advance(state, span, half, half_span, now)
-        span = now
-        give(section, state, span)
-        if after is not None:
-            half, half_span = after[1], after[2]
+    inner = slice(SPAN[0], SPAN[0] + SPAN[1])
+    last = slice(LAST[0], LAST[0] + LAST[1])
+    half[...] = arrive(0, HB, FULL)
+    state[inner] = xbuf[0, inner]
+
+    def step(section, carry):
+        after = arrive(section, 16, SPAN)
+        value = advance(state[inner], half[inner], SPAN)
+        state[inner] = value
+        half[inner] = after
+        give(section - 1, value, SPAN)
+        return carry
+
+    lax.fori_loop(1, NT, step, 0)
+    give(NT - 1, advance(state[last], half[last], LAST), LAST)
 
     frecv[ta] = fsend[ta]
 
@@ -432,6 +441,8 @@
                 pltpu.VMEM((3, ER, LT), jnp.float32),
                 pltpu.VMEM((3, ER, LT), jnp.float32),
                 pltpu.VMEM((9, WR, LT), jnp.float32),
+                pltpu.VMEM((WR, LT), jnp.float32),
+                pltpu.VMEM((WR, LT), jnp.float32),
                 pltpu.VMEM((NT, TR // 2, LT), jnp.float32),
                 pltpu.VMEM((NT, TR // 2, LT), jnp.float32),
                 pltpu.SemaphoreType.DMA((5,)),

time: 21.8 us -> 20.4 us (0.936)
  the two profiles are of different devices: /device:TPU:1 before, /device:TPU:74 now
where the time goes in v4:
time: 20.4 us; the launch traced here: 20.2 us
  Pallas kernels  19.6 us (96%)
  local copies, waits for them, and re-layouts  0.66 us (3%)
    pallas_call x1, Pallas kernels, local(): pl.pallas_call(functools.partial(kernel, gxn, gyn), out_shape=pltpu.VMEM(...  19.6 us
    unnamed x1, local copies, waits for them, and re-layouts  0.66 us

profile of v4, /device:TPU:74, one launch (start us, length us, event | category | flops | bytes accessed | tf_op | source)
XLA Modules:
  0.0 20.2 jit_solution(14328891966778509811)
XLA Ops:
  0.0 19.6 %shard_map.37 = f32[1,64,512]{2,1,0:T(8,128)S(1)} custom-call(f32[1,64,512]{2,1,0:T(8,128)} %u_ref.1, f32[64,512]{1,0:T(8,128)} %cond_ref.1, f32[2,64,512]{2,1,0:T(8,128)} %vel_ref.1), custom_call_target="tpu_custom_call" | custom-call | tf_op jit(solution)/shard_map/pallas_call | solution.py:426
  19.6 0.7 %copy.5 = f32[1,64,512]{2,1,0:T(8,128)} copy(f32[1,64,512]{2,1,0:T(8,128)S(1)} %shard_map.37) | data formatting | bytes 262144

commit v5 on v4

--- a/solution.py
+++ b/solution.py
@@ -15,7 +15,7 @@
 HB = 24
 WR = TR + 2 * HB
 ER = 32
-ROWS = [(0, 0, 24), (1, 7, 16)]
+ROWS = [(0, 0, 18), (1, 4, 16), (5, 7, 8)]
 FULL = (0, WR)
 SPAN = (8, WR - 16)
 LAST = (16, WR - 32)
@@ -107,6 +107,9 @@
     for dy in (-1, 1):
         for dx in (-1, 0, 1):
             count = count + has(dx, dy).astype(jnp.int32)
+
+    xbuf[0, 0:6, :] = jnp.zeros((6, LT), jnp.float32)
+    xbuf[0, WR - 6 : WR, :] = jnp.zeros((6, LT), jnp.float32)
 
     def clear(ref, planes, start, rows):
         ref[:, start : start + rows, :] = jnp.zeros((planes, rows, LT), jnp.float32)
@@ -381,18 +384,20 @@
 
     inner = slice(SPAN[0], SPAN[0] + SPAN[1])
     last = slice(LAST[0], LAST[0] + LAST[1])
-    half[...] = arrive(0, HB, FULL)
+    half[...] = arrive(0, 18, FULL)
     state[inner] = xbuf[0, inner]
 
-    def step(section, carry):
-        after = arrive(section, 16, SPAN)
-        value = advance(state[inner], half[inner], SPAN)
-        state[inner] = value
-        half[inner] = after
-        give(section - 1, value, SPAN)
+    def step(section, carry, halo, span):
+        rows = slice(span[0], span[0] + span[1])
+        after = arrive(section, halo, span)
+        value = advance(state[rows], half[rows], span)
+        state[rows] = value
+        half[rows] = after
+        give(section - 1, value, span)
         return carry
 
-    lax.fori_loop(1, NT, step, 0)
+    lax.fori_loop(1, 5, functools.partial(step, halo=16, span=SPAN), 0)
+    lax.fori_loop(5, NT, functools.partial(step, halo=8, span=LAST), 0)
     give(NT - 1, advance(state[last], half[last], LAST), LAST)
 
     frecv[ta] = fsend[ta]

time: 20.4 us -> 19.9 us (0.975)
  Pallas kernels: 19.6 us -> 19.2 us
    pallas_call x1, Pallas kernels: 19.6 us -> 19.2 us  [local(): pl.pallas_call(functools.partial(kernel, gxn, gyn), out_shape=pltpu.VMEM(...]
where the time goes in v5:
time: 19.9 us; the launch traced here: 19.8 us
  Pallas kernels  19.2 us (96%)
  local copies, waits for them, and re-layouts  0.66 us (3%)
    pallas_call x1, Pallas kernels, local(): pl.pallas_call(functools.partial(kernel, gxn, gyn), out_shape=pltpu.VMEM(...  19.2 us
    unnamed x1, local copies, waits for them, and re-layouts  0.66 us

profile of v5, /device:TPU:74, one launch (start us, length us, event | category | flops | bytes accessed | tf_op | source)
XLA Modules:
  0.0 19.8 jit_solution(18101495399670797267)
XLA Ops:
  0.0 19.2 %shard_map.37 = f32[1,64,512]{2,1,0:T(8,128)S(1)} custom-call(f32[1,64,512]{2,1,0:T(8,128)} %u_ref.1, f32[64,512]{1,0:T(8,128)} %cond_ref.1, f32[2,64,512]{2,1,0:T(8,128)} %vel_ref.1), custom_call_target="tpu_custom_call" | custom-call | tf_op jit(solution)/shard_map/pallas_call | solution.py:431
  19.2 0.7 %copy.5 = f32[1,64,512]{2,1,0:T(8,128)} copy(f32[1,64,512]{2,1,0:T(8,128)S(1)} %shard_map.37) | data formatting | bytes 262144

commit v6 on v5

--- a/solution.py
+++ b/solution.py
@@ -13,9 +13,11 @@
 TC = 512
 LT = 128
 HB = 24
+RAD = 18
+ORDER = (4, 3, 5, 2, 6, 1, 7, 0)
 WR = TR + 2 * HB
 ER = 32
-ROWS = [(0, 0, 18), (1, 4, 16), (5, 7, 8)]
+ROWS = [(0, 0, RAD), (1, 4, 16), (5, 7, 8)]
 FULL = (0, WR)
 SPAN = (8, WR - 16)
 LAST = (16, WR - 32)
@@ -110,6 +112,8 @@
 
     xbuf[0, 0:6, :] = jnp.zeros((6, LT), jnp.float32)
     xbuf[0, WR - 6 : WR, :] = jnp.zeros((6, LT), jnp.float32)
+    cwin[:, 0:6, :] = jnp.zeros((3, 6, LT), jnp.float32)
+    cwin[:, WR - 6 : WR, :] = jnp.zeros((3, 6, LT), jnp.float32)
 
     def clear(ref, planes, start, rows):
         ref[:, start : start + rows, :] = jnp.zeros((planes, rows, LT), jnp.float32)
@@ -199,9 +203,9 @@
     def coef_copy(dx, dy, here=False):
         if dy == 0:
             if dx < 0:
-                src, dst = pl.ds(HB, HB), pl.ds(HB + TR, HB)
+                src, dst = pl.ds(HB, RAD), pl.ds(HB + TR, RAD)
             else:
-                src, dst = pl.ds(TR, HB), pl.ds(0, HB)
+                src, dst = pl.ds(HB + TR - RAD, RAD), pl.ds(HB - RAD, RAD)
             src, dst = cwin.at[:, src, :], cwin.at[:, dst, :]
         else:
             place = pl.ds(*EDGE[dx])
@@ -238,14 +242,14 @@
 
             @pl.when((ta >= first) & (ta <= last))
             def _():
-                for dx in (-1, 1):
-
-                    @pl.when(has(dx, 0))
-                    def _():
-                        for step in range(NT):
+                for step in ORDER:
+                    for dx in (-1, 1):
+
+                        @pl.when(has(dx, 0))
+                        def _():
                             act(strip_copy(ring(step), ta, dx, rows))
 
-        for step in range(1, NT):
+        for step in ORDER[:-1]:
             act(main_copy(ring(step), ta))
 
     sends(lambda copy: copy.start())
@@ -384,7 +388,7 @@
 
     inner = slice(SPAN[0], SPAN[0] + SPAN[1])
     last = slice(LAST[0], LAST[0] + LAST[1])
-    half[...] = arrive(0, 18, FULL)
+    half[...] = arrive(0, RAD, FULL)
     state[inner] = xbuf[0, inner]
 
     def step(section, carry, halo, span):
@@ -402,6 +406,10 @@
 
     frecv[ta] = fsend[ta]
 
+    sends(lambda copy: copy.wait_send())
+    for step in range(1, NT):
+        result_copy(lax.rem(ta + step, NT)).wait_send()
+
     for step in range(1, NT):
         peer = lax.rem(ta + step, NT)
         pltpu.make_async_remote_copy(
@@ -418,10 +426,6 @@
         lanes = slice(tile * LT, (tile + 1) * LT)
         out_ref[0, : TR // 2, lanes] = jnp.where(flane < 64, lower, upper)
         out_ref[0, TR // 2 :, lanes] = roll(jnp.where(flane < 64, upper, lower), 64, 1)
-
-    sends(lambda copy: copy.wait_send())
-    for step in range(1, NT):
-        result_copy(lax.rem(ta + step, NT)).wait_send()
 
 
 def solution(mesh):

time: 19.9 us -> 19.7 us (0.990)
  Pallas kernels: 19.2 us -> 18.9 us
    pallas_call x1, Pallas kernels: 19.2 us -> 18.9 us  [local(): pl.pallas_call(functools.partial(kernel, gxn, gyn), out_shape=pltpu.VMEM(...]
where the time goes in v6:
time: 19.7 us; the launch traced here: 19.6 us
  Pallas kernels  18.9 us (96%)
  local copies, waits for them, and re-layouts  0.66 us (3%)
    pallas_call x1, Pallas kernels, local(): pl.pallas_call(functools.partial(kernel, gxn, gyn), out_shape=pltpu.VMEM(...  18.9 us
    unnamed x1, local copies, waits for them, and re-layouts  0.66 us

profile of v6, /device:TPU:74, one launch (start us, length us, event | category | flops | bytes accessed | tf_op | source)
XLA Modules:
  0.0 19.6 jit_solution(14596321864889554344)
XLA Ops:
  0.0 18.9 %shard_map.37 = f32[1,64,512]{2,1,0:T(8,128)S(1)} custom-call(f32[1,64,512]{2,1,0:T(8,128)} %u_ref.1, f32[64,512]{1,0:T(8,128)} %cond_ref.1, f32[2,64,512]{2,1,0:T(8,128)} %vel_ref.1), custom_call_target="tpu_custom_call" | custom-call | tf_op jit(solution)/shard_map/pallas_call | solution.py:435
  18.9 0.7 %copy.5 = f32[1,64,512]{2,1,0:T(8,128)} copy(f32[1,64,512]{2,1,0:T(8,128)S(1)} %shard_map.37) | data formatting | bytes 262144

commit v7 on v6

--- a/solution.py
+++ b/solution.py
@@ -14,7 +14,7 @@
 LT = 128
 HB = 24
 RAD = 18
-ORDER = (4, 3, 5, 2, 6, 1, 7, 0)
+ORDER = (5, 4, 3, 7, 2, 6, 1, 0)
 WR = TR + 2 * HB
 ER = 32
 ROWS = [(0, 0, RAD), (1, 4, 16), (5, 7, 8)]
@@ -65,6 +65,9 @@
 
     def ring(step):
         return lax.rem(ta + step, NT)
+
+    def mirror(step):
+        return ring(jnp.where(even, step, NT - step))
 
     barrier = pltpu.get_barrier_semaphore()
 
@@ -247,10 +250,10 @@
 
                         @pl.when(has(dx, 0))
                         def _():
-                            act(strip_copy(ring(step), ta, dx, rows))
+                            act(strip_copy(mirror(step), ta, dx, rows))
 
         for step in ORDER[:-1]:
-            act(main_copy(ring(step), ta))
+            act(main_copy(mirror(step), ta))
 
     sends(lambda copy: copy.start())
 

time: 19.7 us -> 19.2 us (0.975)
  Pallas kernels: 18.9 us -> 18.4 us
    pallas_call x1, Pallas kernels: 18.9 us -> 18.4 us  [local(): pl.pallas_call(functools.partial(kernel, gxn, gyn), out_shape=pltpu.VMEM(...]
where the time goes in v7:
time: 19.2 us; the launch traced here: 19.1 us
  Pallas kernels  18.4 us (96%)
  local copies, waits for them, and re-layouts  0.66 us (3%)
    pallas_call x1, Pallas kernels, local(): pl.pallas_call(functools.partial(kernel, gxn, gyn), out_shape=pltpu.VMEM(...  18.4 us
    unnamed x1, local copies, waits for them, and re-layouts  0.66 us

profile of v7, /device:TPU:74, one launch (start us, length us, event | category | flops | bytes accessed | tf_op | source)
XLA Modules:
  0.0 19.1 jit_solution(3170293814827836400)
XLA Ops:
  0.0 18.4 %shard_map.37 = f32[1,64,512]{2,1,0:T(8,128)S(1)} custom-call(f32[1,64,512]{2,1,0:T(8,128)} %u_ref.1, f32[64,512]{1,0:T(8,128)} %cond_ref.1, f32[2,64,512]{2,1,0:T(8,128)} %vel_ref.1), custom_call_target="tpu_custom_call" | custom-call | tf_op jit(solution)/shard_map/pallas_call | solution.py:438
  18.4 0.7 %copy.5 = f32[1,64,512]{2,1,0:T(8,128)} copy(f32[1,64,512]{2,1,0:T(8,128)S(1)} %shard_map.37) | data formatting | bytes 262144

commit v8 on v7

--- a/solution.py
+++ b/solution.py
@@ -234,13 +234,6 @@
                 def _():
                     act(edge_copy(ta, dx, dy))
 
-        for dx, dy, only in coef_dirs:
-            near = has(dx, dy)
-
-            @pl.when(near if only is None else near & (ta == only))
-            def _():
-                act(coef_copy(dx, dy))
-
         for first, last, rows in ROWS:
 
             @pl.when((ta >= first) & (ta <= last))
@@ -251,6 +244,13 @@
                         @pl.when(has(dx, 0))
                         def _():
                             act(strip_copy(mirror(step), ta, dx, rows))
+
+        for dx, dy, only in coef_dirs:
+            near = has(dx, dy)
+
+            @pl.when(near if only is None else near & (ta == only))
+            def _():
+                act(coef_copy(dx, dy))
 
         for step in ORDER[:-1]:
             act(main_copy(mirror(step), ta))

time: 19.2 us -> 19.1 us (level)
  no operation moved by 1% of the time
where the time goes in v8:
time: 19.1 us
  Pallas kernels  18.4 us (96%)
  local copies, waits for them, and re-layouts  0.66 us (3%)
    pallas_call x1, Pallas kernels, local(): pl.pallas_call(functools.partial(kernel, gxn, gyn), out_shape=pltpu.VMEM(...  18.4 us
    unnamed x1, local copies, waits for them, and re-layouts  0.66 us

profile of v8, /device:TPU:74, one launch (start us, length us, event | category | flops | bytes accessed | tf_op | source)
XLA Modules:
  0.0 19.1 jit_solution(9517112388713985695)
XLA Ops:
  0.0 18.4 %shard_map.37 = f32[1,64,512]{2,1,0:T(8,128)S(1)} custom-call(f32[1,64,512]{2,1,0:T(8,128)} %u_ref.1, f32[64,512]{1,0:T(8,128)} %cond_ref.1, f32[2,64,512]{2,1,0:T(8,128)} %vel_ref.1), custom_call_target="tpu_custom_call" | custom-call | tf_op jit(solution)/shard_map/pallas_call | solution.py:438
  18.4 0.7 %copy.5 = f32[1,64,512]{2,1,0:T(8,128)} copy(f32[1,64,512]{2,1,0:T(8,128)S(1)} %shard_map.37) | data formatting | bytes 262144

commit v9 on v8

--- a/solution.py
+++ b/solution.py
@@ -252,7 +252,7 @@
             def _():
                 act(coef_copy(dx, dy))
 
-        for step in ORDER[:-1]:
+        for step in (4, 5, 3, 7, 2, 6, 1):
             act(main_copy(mirror(step), ta))
 
     sends(lambda copy: copy.start())

time: 19.1 us -> 19.1 us (level)
  no operation moved by 1% of the time
where the time goes in v9:
time: 19.1 us
  Pallas kernels  18.4 us (96%)
  local copies, waits for them, and re-layouts  0.66 us (3%)
    pallas_call x1, Pallas kernels, local(): pl.pallas_call(functools.partial(kernel, gxn, gyn), out_shape=pltpu.VMEM(...  18.4 us
    unnamed x1, local copies, waits for them, and re-layouts  0.66 us

profile of v9, /device:TPU:74, one launch (start us, length us, event | category | flops | bytes accessed | tf_op | source)
XLA Modules:
  0.0 19.1 jit_solution(11930756851917668055)
XLA Ops:
  0.0 18.4 %shard_map.37 = f32[1,64,512]{2,1,0:T(8,128)S(1)} custom-call(f32[1,64,512]{2,1,0:T(8,128)} %u_ref.1, f32[64,512]{1,0:T(8,128)} %cond_ref.1, f32[2,64,512]{2,1,0:T(8,128)} %vel_ref.1), custom_call_target="tpu_custom_call" | custom-call | tf_op jit(solution)/shard_map/pallas_call | solution.py:438
  18.4 0.7 %copy.5 = f32[1,64,512]{2,1,0:T(8,128)} copy(f32[1,64,512]{2,1,0:T(8,128)S(1)} %shard_map.37) | data formatting | bytes 262144

commit v10 on v9

--- a/solution.py
+++ b/solution.py
@@ -14,7 +14,7 @@
 LT = 128
 HB = 24
 RAD = 18
-ORDER = (5, 4, 3, 7, 2, 6, 1, 0)
+ORDER = (4, 5, 3, 7, 2, 6, 1, 0)
 WR = TR + 2 * HB
 ER = 32
 ROWS = [(0, 0, RAD), (1, 4, 16), (5, 7, 8)]

time: 19.1 us -> 19.1 us (level)
  no operation moved by 1% of the time
where the time goes in v10:
time: 19.1 us
  Pallas kernels  18.4 us (96%)
  local copies, waits for them, and re-layouts  0.66 us (3%)
    pallas_call x1, Pallas kernels, local(): pl.pallas_call(functools.partial(kernel, gxn, gyn), out_shape=pltpu.VMEM(...  18.4 us
    unnamed x1, local copies, waits for them, and re-layouts  0.66 us

profile of v10, /device:TPU:74, one launch (start us, length us, event | category | flops | bytes accessed | tf_op | source)
XLA Modules:
  0.0 19.1 jit_solution(14713121794549692104)
XLA Ops:
  0.0 18.4 %shard_map.37 = f32[1,64,512]{2,1,0:T(8,128)S(1)} custom-call(f32[1,64,512]{2,1,0:T(8,128)} %u_ref.1, f32[64,512]{1,0:T(8,128)} %cond_ref.1, f32[2,64,512]{2,1,0:T(8,128)} %vel_ref.1), custom_call_target="tpu_custom_call" | custom-call | tf_op jit(solution)/shard_map/pallas_call | solution.py:438
  18.4 0.7 %copy.5 = f32[1,64,512]{2,1,0:T(8,128)} copy(f32[1,64,512]{2,1,0:T(8,128)S(1)} %shard_map.37) | data formatting | bytes 262144
